TPU v7x, 512 devices: a whole 4x8x8 slice. The times are simulated.
512 devices in a mesh: seq: 128 (over y, z, core), win: 4 (over x).
Axes of the slice: x: 4, y: 8, z: 8, core: 2. Of those that a mesh axis runs over, the one named last changes fastest.
Arguments:
- queries: bfloat16 [65536, 1024], P(('win', 'seq')), parts along dimension 0, may hold values from -6 to 6
- key_rows: bfloat16 [65536, 1024], P(('win', 'seq')), parts along dimension 0, may hold values from -6 to 6
- value_rows: bfloat16 [65536, 2048], P(('win', 'seq')), parts along dimension 0, may hold values from -6 to 6
- residual: bfloat16 [65536, 1024], P(('win', 'seq')), parts along dimension 0, may hold values from -6 to 6
- out_weight: bfloat16 [2048, 1024], P(None, 'seq'), may hold values from -0.125 to 0.125
- expert_in: bfloat16 [128, 1024, 768], P('seq'), may hold values from -0.1875 to 0.1875
- expert_out: bfloat16 [128, 384, 1024], P('seq'), may hold values from -0.3125 to 0.3125
- expert_ids: int32 [65536, 2], P(('win', 'seq')), parts along dimension 0, may hold values from 0 to 127, all different within a row; in each aligned block of 128 rows (0 to 127, 128 to 255, ...) at most 4 rows name the same one
- gate_values: float32 [65536, 2], P(('win', 'seq')), parts along dimension 0, may hold values from 0.2 to 1
Outputs:
- layer_out: bfloat16 [65536, 1024], P(('win', 'seq')), parts along dimension 0
There are 4 independent parts, one for each index of `win`. A program takes and returns all parts, laid end to end along the dimension named above; an argument that names none is the same for every part. Nothing has to cross between parts.
Inputs may be any that keep to these rules, and one draw needn't show every extreme that they name: `expert_ids`: the 2 ids of a row differ. Within the rows of one block of 128 tokens no expert is named by more than 4 rows, a bound that some block reaches. Every expert is named somewhere.
All inputs are finite; a program needn't handle non-finite values.
Results may differ from a plain program's by a relative error of at most 0.013.
Values may be sent and summed in bfloat16 or wider, within the bound.
A program may use at most 128 MiB of HBM per device.

v0:
```python
import jax
import jax.numpy as jnp
from jax import lax
from jax.sharding import PartitionSpec as P

D = 1024
H = 16
DK = 64
DV = 128
HE = 384
TOP = 2


def carried_in(x, axis, join, neutral):
    place = lax.axis_index(axis)
    gathered = lax.all_gather(x.astype(jnp.bfloat16), axis)
    state = jnp.zeros_like(x) + jnp.asarray(neutral, x.dtype)

    def one(step, state):
        return join(state, lax.dynamic_index_in_dim(gathered, step, 0, False).astype(x.dtype))

    return lax.fori_loop(0, place, one, state)


def add_states(earlier, later):
    return earlier + later


def per_device(
    queries,
    key_rows,
    value_rows,
    residual,
    out_weight,
    expert_in,
    expert_out,
    expert_ids,
    gate_values,
):
    length = queries.shape[0]
    q_heads = queries.reshape(length, H, DK)
    k_heads = key_rows.reshape(length, H, DK)
    v_heads = value_rows.reshape(length, H, DV)
    local_state = jnp.einsum("thd,the->hde", k_heads, v_heads, preferred_element_type=jnp.float32)
    prefix = carried_in(local_state, "seq", add_states, jnp.zeros_like(local_state))
    causal = jnp.arange(length)[:, None] >= jnp.arange(length)[None, :]
    scores = jnp.einsum("thd,shd->hts", q_heads, k_heads, preferred_element_type=jnp.float32)
    scores = jnp.where(causal[None], scores, 0.0).astype(jnp.bfloat16)
    intra_sum = jnp.einsum("hts,she->the", scores, v_heads, preferred_element_type=jnp.float32)
    inter_sum = jnp.einsum(
        "thd,hde->the", q_heads.astype(jnp.float32), prefix, precision=lax.Precision.HIGHEST
    )
    position = (lax.axis_index("seq") * length + jnp.arange(length)).astype(jnp.float32)
    scaling = lax.rsqrt((position + 1.0) * DK)
    attended = (
        ((intra_sum + inter_sum) * scaling[:, None, None])
        .astype(jnp.bfloat16)
        .reshape(length, H * DV)
    )
    projected = jnp.dot(
        attended,
        lax.all_gather(out_weight, "seq", axis=1, tiled=True),
        preferred_element_type=jnp.float32,
    )
    hidden = (residual.astype(jnp.float32) + projected).astype(jnp.bfloat16)
    hidden_float = hidden.astype(jnp.float32)
    normed = (
        hidden_float
        * lax.rsqrt(jnp.mean(hidden_float * hidden_float, axis=-1, keepdims=True) + 1e-06)
    ).astype(jnp.bfloat16)
    experts = lax.axis_size("seq") * expert_in.shape[0]
    capacity = max(2, 2 * length * TOP // experts)
    flat_ids = expert_ids.reshape(-1)
    one_hot = (flat_ids[:, None] == jnp.arange(experts)[None, :]).astype(jnp.int32)
    earlier = jnp.cumsum(one_hot, axis=0) - one_hot
    slot_index = jnp.sum(earlier * one_hot, axis=-1)
    dest_row = flat_ids * capacity + slot_index
    buffer = (
        jnp.zeros((experts * capacity, D), jnp.bfloat16)
        .at[dest_row]
        .set(jnp.repeat(normed, TOP, axis=0))
    )
    buffer = buffer.reshape(experts, 1, capacity, D)
    act = jnp.einsum(
        "ensd,edf->ensf",
        lax.all_to_all(buffer, "seq", split_axis=0, concat_axis=1, tiled=True),
        expert_in,
        preferred_element_type=jnp.float32,
    )
    inner = (jax.nn.silu(act[..., :HE]) * act[..., HE:]).astype(jnp.bfloat16)
    produced_all = jnp.einsum(
        "ensf,efd->ensd", inner, expert_out, preferred_element_type=jnp.float32
    ).astype(jnp.bfloat16)
    returned_rows = lax.all_to_all(produced_all, "seq", split_axis=1, concat_axis=0, tiled=True)
    picked = returned_rows.reshape(experts * capacity, D)[dest_row]
    combined = jnp.sum(
        picked.astype(jnp.float32).reshape(length, TOP, D) * gate_values[:, :, None], axis=1
    )
    return (hidden_float + combined).astype(jnp.bfloat16)


def solution(mesh):
    in_specs = (
        P(("win", "seq"), None),
        P(("win", "seq"), None),
        P(("win", "seq"), None),
        P(("win", "seq"), None),
        P(None, "seq"),
        P("seq", None, None),
        P("seq", None, None),
        P(("win", "seq"), None),
        P(("win", "seq"), None),
    )
    out_specs = P(("win", "seq"), None)
    return jax.shard_map(
        per_device, mesh=mesh, in_specs=in_specs, out_specs=out_specs, check_vma=False
    )
```

profile of v0, /device:TPU:2, one launch (start us, length us, event | category | flops | bytes accessed | tf_op | source)
XLA Modules:
  0.0 401.8 jit_solution(2190676096343332066)
XLA Ops:
  6.5 1.2 copy.28
  7.8 2.0 convolution_convert_fusion.1
  9.9 0.7 all-gather.4.cloned.1.call-update
  11.3 0.2 fusion.26
  12.1 1.7 convolution_bitcast_fusion.1
  13.9 142.8 %all-gather.6.cloned.1.call-done = bf16[2048,64,128]{2,1,0:T(8,128)(2,1)} async-done(((bf16[16,64,128]{2,1,0:T(8,128)(2,1)}), bf16[2048,64,128]{2,1,0:T(8,128)(2,1)}) %all-gather.6.cloned.1.call-update) | async-done | bytes 33554448 | tf_op jit(solution)/shard_map/all_gather | solution.py:16
  156.8 1.8 fusion.8
  158.6 83.9 %all-gather.4.cloned.1.call-done = bf16[2048,1024]{0,1:T(8,128)(2,1)} async-done(((bf16[2048,8]{0,1:T(8,128)(2,1)}), bf16[2048,1024]{0,1:T(8,128)(2,1)}) %all-gather.4.cloned.1.call-update) | async-done | bytes 4194320 | tf_op jit(solution)/shard_map/all_gather | solution.py:62
  242.4 4.0 multiply_reduce_fusion.1
  246.5 0.3 broadcast_in_dim.34
  246.8 1.0 reshape.151
  247.8 2.4 scatter_custom_fusion
  250.2 1.2 reshape.131
  251.4 94.1 %all_to_all.8 = bf16[128,1,4,1024]{3,2,1,0:T(4,128)(2,1)S(1)} all-to-all(bf16[128,1,4,1024]{3,2,1,0:T(4,128)(2,1)} %bitcast.76), channel_id=1, replica_groups=mesh['seq'=128,'win'=4] {'seq'}, dimensions={0} | all-to-all | bytes 2097152 | tf_op jit(solution)/shard_map/all_to_all | solution.py:86
  345.5 1.4 fusion.2
  346.9 0.7 fusion.5
  347.6 1.8 copy.38
  349.5 7.6 %all-to-all-start.1 = ((bf16[1,128,4,1024]{3,2,0,1:T(4,128)(2,1)}), bf16[1,128,4,1024]{3,2,0,1:T(4,128)(2,1)}, u32[]{:S(2)}, u32[]{:S(2)}) async-start(bf16[1,128,4,1024]{3,2,0,1:T(4,128)(2,1)} %copy.38), calls=%async_computation.1 | async-start | bytes 2097152 | tf_op jit(solution)/shard_map/all_to_all | solution.py:94
  357.3 30.5 %all-to-all-done.1 = bf16[1,128,4,1024]{3,2,0,1:T(4,128)(2,1)} async-done(((bf16[1,128,4,1024]{3,2,0,1:T(4,128)(2,1)}), bf16[1,128,4,1024]{3,2,0,1:T(4,128)(2,1)}, u32[]{:S(2)}, u32[]{:S(2)}) %all-to-all-start.1) | async-done | bytes 1048608 | tf_op jit(solution)/shard_map/all_to_all | solution.py:94
  387.8 1.3 reshape.136
  389.1 2.0 gather_fusion
  391.1 1.7 reshape.138
  392.8 1.3 multiply_reduce_fusion
  394.1 0.8 add_convert_fusion
  (37 shorter events, 1.6 us)
Async XLA Ops:
  6.5 339.0 %copy-start = (bf16[1,1024,768]{2,1,0:T(8,128)(2,1)S(1)}, bf16[1,1024,768]{2,1,0:T(8,128)(2,1)}, u32[]{:S(2)}) copy-start(bf16[1,1024,768]{2,1,0:T(8,128)(2,1)} %param.16) | copy-start | bytes 4718596
  6.5 4.1 %copy-start.2 = (s32[128,2]{0,1:T(2,128)S(1)}, s32[128,2]{0,1:T(2,128)}, u32[]{:S(2)}) copy-start(s32[128,2]{0,1:T(2,128)} %param.18) | copy-start | bytes 3076
  6.5 4.5 %copy-start.1 = (bf16[128,1024]{1,0:T(8,128)(2,1)S(1)}, bf16[128,1024]{1,0:T(8,128)(2,1)}, u32[]{:S(2)}) copy-start(bf16[128,1024]{1,0:T(8,128)(2,1)} %param.11) | copy-start | bytes 786436
  6.5 150.1 %all-gather.6.cloned.1.call-start = ((), (), s32[]{:S(2)}) async-start(), calls=%async_computation.3 | async-start | bytes 33816576 | tf_op jit(solution)/shard_map/all_gather | solution.py:16
  9.8 232.6 %all-gather.4.cloned.1.call-start = ((), (), s32[]{:S(2)}) async-start(), calls=%async_computation.2 | async-start | bytes 4227072 | tf_op jit(solution)/shard_map/all_gather | solution.py:62
  345.5 1.4 copy-start.4
  349.5 7.6 %copy-start.3 = (f32[128,2]{0,1:T(2,128)S(1)}, f32[128,2]{0,1:T(2,128)}, u32[]{:S(2)}) copy-start(f32[128,2]{0,1:T(2,128)} %param.19) | copy-start | bytes 3076
  349.5 38.3 %all-to-all-start.1 = ((bf16[1,128,4,1024]{3,2,0,1:T(4,128)(2,1)}), bf16[1,128,4,1024]{3,2,0,1:T(4,128)(2,1)}, u32[]{:S(2)}, u32[]{:S(2)}) async-start(bf16[1,128,4,1024]{3,2,0,1:T(4,128)(2,1)} %copy.38), calls=%async_computation.1 | async-start | bytes 2097152 | tf_op jit(solution)/shard_map/all_to_all | solution.py:94
Sparse Core Ops, SparseCore 0:
  10.5 146.1 all-gather.5
  159.8 82.5 all-gather.3
where the time goes:
time: 406 us; the launch traced here: 402 us
  waiting for transfers between devices  258 us (64%)
  blocking collectives  94.1 us (23%)
  local copies, waits for them, and re-layouts  14.1 us (3%)
  between operations  13.6 us (3%)
  matrix products  11.6 us (3%)
  starting transfers between devices  7.67 us (2%)
    all_gather x1, waiting for transfers between devices, carried_in(): gathered = lax.all_gather(x.astype(jnp.bfloat16), axis)  143 us
    all_to_all x1, blocking collectives, per_device(): lax.all_to_all(buffer, 'seq', split_axis=0, concat_axis=1, tiled=True)  94.1 us
    all_gather x1, waiting for transfers between devices, per_device(): lax.all_gather(out_weight, 'seq', axis=1, tiled=True)  83.9 us
    all_to_all x1, waiting for transfers between devices, per_device(): lax.all_to_all(produced_all, 'seq', split_axis=1, concat_axis=0, tiled=True)  30.5 us
  transfers between devices with their start and end apart: 3, of which 3 were waited for; matrix products, arithmetic and copies ran while one was open for 1% of the time, Pallas kernels for 0%

commit v1 on v0

--- a/solution.py
+++ b/solution.py
@@ -59,7 +59,12 @@
     )
     projected = jnp.dot(
         attended,
-        lax.all_gather(out_weight, "seq", axis=1, tiled=True),
+        jnp.concatenate(
+            lax.all_to_all(
+                jnp.stack([out_weight for _ in range(lax.axis_size("seq"))], axis=0), "seq", 0, 0
+            ),
+            axis=1,
+        ),
         preferred_element_type=jnp.float32,
     )
     hidden = (residual.astype(jnp.float32) + projected).astype(jnp.bfloat16)

time: 406 us -> 491 us (1.21)
  blocking collectives: 94.1 us -> 177 us
  waiting for transfers between devices: 258 us -> 238 us
  starting transfers between devices: 7.67 us -> 25.8 us
    all_gather x1 -> x0, waiting for transfers between devices: 83.9 us -> none  [per_device(): lax.all_gather(out_weight, 'seq', axis=1, tiled=True)]
    all_to_all x1, blocking collectives: 94.1 us -> 177 us  [per_device(): lax.all_to_all(buffer, 'seq', split_axis=0, concat_axis=1, tiled=True)]
    all_gather x1, waiting for transfers between devices: 143 us -> 208 us  [carried_in(): gathered = lax.all_gather(x.astype(jnp.bfloat16), axis)]
    all_to_all x0 -> x1, starting transfers between devices: none -> 18.5 us  [per_device(): lax.all_to_all(jnp.stack([out_weight for _ in range(lax.axis_size('seq'))...]
  transfers between devices with their start and end apart: 3 -> 3, of which waited for: 3 -> 2; matrix products, arithmetic and copies ran while one was open for 1% -> 2% of each run, Pallas kernels for 0% -> 0%
where the time goes in v1:
time: 491 us; the launch traced here: 487 us
  waiting for transfers between devices  238 us (48%)
  blocking collectives  177 us (36%)
  starting transfers between devices  25.8 us (5%)
  local copies, waits for them, and re-layouts  17.3 us (4%)
  between operations  13.6 us (3%)
  matrix products  11.6 us (2%)
    all_gather x1, waiting for transfers between devices, carried_in(): gathered = lax.all_gather(x.astype(jnp.bfloat16), axis)  208 us
    all_to_all x1, blocking collectives, per_device(): lax.all_to_all(buffer, 'seq', split_axis=0, concat_axis=1, tiled=True)  177 us
    all_to_all x1, waiting for transfers between devices, per_device(): lax.all_to_all(produced_all, 'seq', split_axis=1, concat_axis=0, tiled=True)  30.5 us
    all_to_all x1, starting transfers between devices, per_device(): lax.all_to_all(jnp.stack([out_weight for _ in range(lax.axis_size('seq'))...  18.5 us
  transfers between devices with their start and end apart: 3, of which 2 were waited for; matrix products, arithmetic and copies ran while one was open for 2% of the time, Pallas kernels for 0%

profile of v1, /device:TPU:2, one launch (start us, length us, event | category | flops | bytes accessed | tf_op | source)
XLA Modules:
  0.0 486.6 jit_solution(1595529695661910814)
XLA Ops:
  6.5 1.2 copy.29
  7.8 2.0 convolution_convert_fusion.1
  9.8 3.2 stack.2
  13.1 18.5 %all-to-all-start = ((bf16[128,2048,8]{1,2,0:T(8,128)(2,1)}), bf16[128,2048,8]{1,2,0:T(8,128)(2,1)}, u32[]{:S(2)}, u32[]{:S(2)}) async-start(bf16[128,2048,8]{1,2,0:T(8,128)(2,1)} %stack.2), calls=%async_computation | async-start | bytes 8388608 | tf_op jit(solution)/shard_map/all_to_all | solution.py:63
  32.3 0.2 fusion.35
  33.1 1.7 convolution_bitcast_fusion.1
  34.8 207.7 %all-gather.3.cloned.1.call-done = bf16[2048,64,128]{2,1,0:T(8,128)(2,1)} async-done(((bf16[16,64,128]{2,1,0:T(8,128)(2,1)}), bf16[2048,64,128]{2,1,0:T(8,128)(2,1)}) %all-gather.3.cloned.1.call-update) | async-done | bytes 33554448 | tf_op jit(solution)/shard_map/all_gather | solution.py:16
  242.5 1.8 fusion.10
  244.3 4.0 multiply_reduce_fusion.1
  248.4 0.3 broadcast_in_dim.34
  248.7 1.0 reshape.161
  249.7 2.4 scatter_custom_fusion
  252.1 1.2 reshape.141
  253.3 177.4 %all_to_all.23 = bf16[128,1,4,1024]{3,2,1,0:T(4,128)(2,1)S(1)} all-to-all(bf16[128,1,4,1024]{3,2,1,0:T(4,128)(2,1)} %bitcast.89), channel_id=1, replica_groups=mesh['seq'=128,'win'=4] {'seq'}, dimensions={0} | all-to-all | bytes 2097152 | tf_op jit(solution)/shard_map/all_to_all | solution.py:91
  430.7 1.4 fusion.4
  432.1 0.7 fusion.7
  432.8 1.8 copy.39
  434.7 7.3 %all-to-all-start.2 = ((bf16[1,128,4,1024]{3,2,0,1:T(4,128)(2,1)}), bf16[1,128,4,1024]{3,2,0,1:T(4,128)(2,1)}, u32[]{:S(2)}, u32[]{:S(2)}) async-start(bf16[1,128,4,1024]{3,2,0,1:T(4,128)(2,1)} %copy.39), calls=%async_computation.2 | async-start | bytes 2097152 | tf_op jit(solution)/shard_map/all_to_all | solution.py:99
  442.1 30.5 %all-to-all-done.2 = bf16[1,128,4,1024]{3,2,0,1:T(4,128)(2,1)} async-done(((bf16[1,128,4,1024]{3,2,0,1:T(4,128)(2,1)}), bf16[1,128,4,1024]{3,2,0,1:T(4,128)(2,1)}, u32[]{:S(2)}, u32[]{:S(2)}) %all-to-all-start.2) | async-done | bytes 1048608 | tf_op jit(solution)/shard_map/all_to_all | solution.py:99
  472.6 1.3 reshape.146
  474.0 2.0 gather_fusion
  475.9 1.7 reshape.148
  477.6 1.3 multiply_reduce_fusion
  479.0 0.8 add_convert_fusion
  (37 shorter events, 1.5 us)
Async XLA Ops:
  6.5 424.2 %copy-start = (bf16[1,1024,768]{2,1,0:T(8,128)(2,1)S(1)}, bf16[1,1024,768]{2,1,0:T(8,128)(2,1)}, u32[]{:S(2)}) copy-start(bf16[1,1024,768]{2,1,0:T(8,128)(2,1)} %param.16) | copy-start | bytes 4718596
  6.5 235.9 %all-gather.3.cloned.1.call-start = ((), (), s32[]{:S(2)}) async-start(), calls=%async_computation.3 | async-start | bytes 33816576 | tf_op jit(solution)/shard_map/all_gather | solution.py:16
  13.1 18.5 %copy-start.2 = (s32[128,2]{0,1:T(2,128)S(1)}, s32[128,2]{0,1:T(2,128)}, u32[]{:S(2)}) copy-start(s32[128,2]{0,1:T(2,128)} %param.18) | copy-start | bytes 3076
  13.1 19.6 %copy-start.1 = (bf16[128,1024]{1,0:T(8,128)(2,1)S(1)}, bf16[128,1024]{1,0:T(8,128)(2,1)}, u32[]{:S(2)}) copy-start(bf16[128,1024]{1,0:T(8,128)(2,1)} %param.11) | copy-start | bytes 786436
  13.1 231.3 %all-to-all-start = ((bf16[128,2048,8]{1,2,0:T(8,128)(2,1)}), bf16[128,2048,8]{1,2,0:T(8,128)(2,1)}, u32[]{:S(2)}, u32[]{:S(2)}) async-start(bf16[128,2048,8]{1,2,0:T(8,128)(2,1)} %stack.2), calls=%async_computation | async-start | bytes 8388608 | tf_op jit(solution)/shard_map/all_to_all | solution.py:63
  430.7 1.4 copy-start.4
  432.8 9.2 %copy-start.3 = (f32[128,2]{0,1:T(2,128)S(1)}, f32[128,2]{0,1:T(2,128)}, u32[]{:S(2)}) copy-start(f32[128,2]{0,1:T(2,128)} %param.19) | copy-start | bytes 3076
  434.7 38.0 %all-to-all-start.2 = ((bf16[1,128,4,1024]{3,2,0,1:T(4,128)(2,1)}), bf16[1,128,4,1024]{3,2,0,1:T(4,128)(2,1)}, u32[]{:S(2)}, u32[]{:S(2)}) async-start(bf16[1,128,4,1024]{3,2,0,1:T(4,128)(2,1)} %copy.39), calls=%async_computation.2 | async-start | bytes 2097152 | tf_op jit(solution)/shard_map/all_to_all | solution.py:99
Sparse Core Ops, SparseCore 0:
  10.5 231.9 all-gather.2
